TPU v7x, 32 devices: a whole 2x2x4 slice. The times are simulated.
32 devices in a mesh: patch: 2 (over y), exp: 4 (over z), strip: 2 (over x), band: 2 (over core).
Axes of the slice: x: 2, y: 2, z: 4, core: 2. Of those that a mesh axis runs over, the one named last changes fastest.
Arguments:
- images: float32 [64, 64, 512], P(('patch', 'exp'), 'strip', 'band'), parts along dimension 0, may hold values from -80 to 80
- valid_mask: int32 [64, 64, 512], P(('patch', 'exp'), 'strip', 'band'), parts along dimension 0, may hold values from 0 to 1, as said below
- basis_index: int32 [64, 4, 2], P(('patch', 'exp'), 'strip'), parts along dimension 0, may hold values from 0 to 15
- match_index: int32 [64, 4, 2], P(('patch', 'exp'), 'strip'), parts along dimension 0, may hold values from 0 to 15
- psf_bank: float32 [16, 81], replicated, may hold values from 0.05 to 1
Outputs:
- coadd_image: float32 [128, 512], P(('patch', 'strip'), 'band'), parts along dimension 0
- difference: float32 [64, 64, 512], P(('patch', 'exp'), 'strip', 'band'), parts along dimension 0
There are 2 independent parts, one for each index of `patch`. A program takes and returns all parts, laid end to end along the dimension named above; an argument that names none is the same for every part. Nothing has to cross between parts.
Inputs may be any that keep to these rules, and one draw needn't show every extreme that they name: `valid_mask`: one marks a valid pixel of that exposure.
All inputs are finite; a program needn't handle non-finite values.
Results may differ from a plain program's by a relative error of at most 0.0003.
Values sent between devices are 32-bit elements; how exact they have to be, the bound alone decides.
A program may use at most 128 MiB of HBM per device.

v0:
```python
import jax
import jax.numpy as jnp
from jax import lax
from jax.sharding import PartitionSpec as P

TILE_ROWS = 16
KERNEL = 9


sentinel = 1e30


def extended(cells, sides, width):
    for axis, dim in sides:
        count = lax.axis_size(axis)
        ends = count - 1
        head = lax.slice_in_dim(cells, 0, width, axis=dim)
        tail = lax.slice_in_dim(cells, cells.shape[dim] - width, cells.shape[dim], axis=dim)
        cells = jnp.concatenate(
            [
                lax.ppermute(tail, axis, [(i, (i + 1) % count) for i in range(ends)]),
                cells,
                lax.ppermute(head, axis, [((i + 1) % count, i) for i in range(ends)]),
            ],
            axis=dim,
        )
    return cells


def joined(value, axis, join):
    pieces = jax.tree.map(lambda part: lax.all_gather(part, axis), value)
    head = jax.tree.map(lambda part: part[0], pieces)
    tail = jax.tree.map(lambda part: part[1:], pieces)
    total, _ = lax.scan(lambda total, section: (join(total, section), None), head, tail)
    return total


def vary_conv(padded, kernels, blend_map):
    row_count = kernels.shape[-3]
    col_count = blend_map.shape[0]
    low_acc = jnp.zeros(kernels.shape[:-2] + (col_count,), jnp.float32)
    high_acc = jnp.zeros(kernels.shape[:-2] + (col_count,), jnp.float32)
    for row_off in range(KERNEL):
        for col_off in range(KERNEL):
            window = padded[..., row_off : row_off + row_count, col_off : col_off + col_count]
            tap_at = row_off * KERNEL + col_off
            low_acc = low_acc + kernels[..., 0, tap_at][..., None] * window
            high_acc = high_acc + kernels[..., 1, tap_at][..., None] * window
    return (1.0 - blend_map) * low_acc + blend_map * high_acc


def tile_kernels(tile_index, psf_bank):
    normed = psf_bank / jnp.sum(psf_bank, axis=1, keepdims=True)
    onehot = (tile_index[..., None] == jnp.arange(psf_bank.shape[0], dtype=jnp.int32)).astype(
        jnp.float32
    )
    kernels = jnp.einsum("etkb,bq->etkq", onehot, normed, precision=lax.Precision.HIGHEST)
    return jnp.repeat(kernels, TILE_ROWS, axis=1)


def member(stacked, position):
    return lax.index_in_dim(stacked, position, axis=stacked.ndim - 3, keepdims=False)


def lower_three(first_set, second_set):
    a_zero, a_one, a_two = (member(first_set, 0), member(first_set, 1), member(first_set, 2))
    b_zero, b_one, b_two = (member(second_set, 0), member(second_set, 1), member(second_set, 2))
    first = jnp.minimum(a_zero, b_zero)
    second = jnp.minimum(jnp.minimum(a_one, b_one), jnp.maximum(a_zero, b_zero))
    third = jnp.minimum(
        jnp.minimum(a_two, b_two),
        jnp.minimum(jnp.maximum(a_one, b_zero), jnp.maximum(a_zero, b_one)),
    )
    return jnp.stack([first, second, third], axis=-3)


def upper_three(first_set, second_set):
    a_zero, a_one, a_two = (member(first_set, 0), member(first_set, 1), member(first_set, 2))
    b_zero, b_one, b_two = (member(second_set, 0), member(second_set, 1), member(second_set, 2))
    first = jnp.maximum(a_zero, b_zero)
    second = jnp.maximum(jnp.maximum(a_one, b_one), jnp.minimum(a_zero, b_zero))
    third = jnp.maximum(
        jnp.maximum(a_two, b_two),
        jnp.maximum(jnp.minimum(a_one, b_zero), jnp.minimum(a_zero, b_one)),
    )
    return jnp.stack([first, second, third], axis=-3)


def combine(left_stats, right_stats):
    return (
        left_stats[0] + right_stats[0],
        left_stats[1] + right_stats[1],
        lower_three(left_stats[2], right_stats[2]),
        upper_three(left_stats[3], right_stats[3]),
    )


def tree_fold(statistics):
    while statistics[0].shape[0] > 1:
        length_now = statistics[0].shape[0]
        split_at = length_now // 2
        front_part = tuple((entry[:split_at] for entry in statistics))
        back_part = tuple((entry[split_at : 2 * split_at] for entry in statistics))
        merged = combine(front_part, back_part)
        statistics = merged
    return tuple((entry[0] for entry in statistics))


def finish(statistics):
    total_sum = statistics[0]
    valid_count = statistics[1]
    low_three, high_three = (statistics[2], statistics[3])
    low_sum = member(low_three, 0) + member(low_three, 1) + member(low_three, 2)
    high_sum = member(high_three, 0) + member(high_three, 1) + member(high_three, 2)
    return (total_sum - low_sum - high_sum) / (valid_count - 6.0)


def on_device(images, valid_mask, basis_index, match_index, psf_bank):
    rim_width = KERNEL // 2
    col_count = images.shape[2]
    columns = lax.axis_index("band") * col_count + jnp.arange(col_count, dtype=jnp.int32)
    blend_map = columns.astype(jnp.float32) / (col_count * lax.axis_size("band") - 1)
    image_padded = extended(images, (("strip", 1), ("band", 2)), rim_width)
    warped = vary_conv(image_padded, tile_kernels(basis_index, psf_bank), blend_map)
    is_valid = valid_mask == 1
    filler = jnp.full(warped.shape, sentinel, jnp.float32)
    low_start = jnp.stack([jnp.where(is_valid, warped, sentinel), filler, filler], axis=1)
    high_start = jnp.stack([jnp.where(is_valid, warped, -sentinel), -filler, -filler], axis=1)
    local_stats = tree_fold(
        (jnp.where(is_valid, warped, 0.0), valid_mask.astype(jnp.float32), low_start, high_start)
    )
    total_stats = joined(local_stats, "exp", combine)
    coadd_image = finish(total_stats)
    coadd_padded = extended(coadd_image, (("strip", 0), ("band", 1)), rim_width)
    matched = vary_conv(coadd_padded, tile_kernels(match_index, psf_bank), blend_map)
    return (coadd_image, images - matched)


def solution(mesh):
    return jax.shard_map(
        on_device,
        mesh=mesh,
        in_specs=(
            P(("patch", "exp"), "strip", "band"),
            P(("patch", "exp"), "strip", "band"),
            P(("patch", "exp"), "strip", None),
            P(("patch", "exp"), "strip", None),
            P(),
        ),
        out_specs=(P(("patch", "strip"), "band"), P(("patch", "exp"), "strip", "band")),
        check_vma=False,
    )
```

profile of v0, /device:TPU:0, one launch (start us, length us, event | category | flops | bytes accessed | tf_op | source)
XLA Modules:
  0.0 134.9 jit_solution(10140037247067433031)
XLA Ops:
  1.5 4.8 %collective-permute-start = (f32[8,4,256]{2,1,0:T(4,128)S(1)}, f32[8,4,256]{2,1,0:T(4,128)S(1)}, u32[]{:S(2)}, u32[]{:S(2)}) collective-permute-start(f32[8,4,256]{2,1,0:T(4,128)S(1)} %get-tuple-element.428), channel_id=1, source_target_pairs={{0,2},{1,3},{4,6},{5,7},{8,10},{9,11},{12,14},{13,15},{16,18},{17,... | collective-permute-start | bytes 98312 | tf_op jit(solution)/shard_map/ppermute | solution.py:21
  10.8 1.4 %slice_reduce_fusion.195 = (f32[8,32]{1,0:T(8,128)S(1)}, f32[8,32]{1,0:T(8,128)S(1)}, f32[8,32]{1,0:T(8,128)S(1)}, f32[8,32]{1,0:T(8,128)S(1)}, f32[8,32]{1,0:T(...) fusion(f32[8,32,2,81]{3,1,2,0:T(8,128)S(1)} %bitcast.96), kind=kLoop, calls=%fused_computation.230 | loop fusion | bytes 38912 | tf_op jit(solution)/shard_map/slice | solution.py:48
  12.2 1.4 %slice_reduce_fusion.318 = (f32[8,32]{1,0:T(8,128)S(1)}, f32[8,32]{1,0:T(8,128)S(1)}, f32[8,32]{1,0:T(8,128)S(1)}, f32[8,32]{1,0:T(8,128)S(1)}, f32[8,32]{1,0:T(...) fusion(f32[8,32,2,81]{3,1,2,0:T(8,128)S(1)} %bitcast.97), kind=kLoop, calls=%fused_computation.353 | loop fusion | bytes 38912 | tf_op jit(solution)/shard_map/slice | solution.py:47
  13.6 1.4 %slice_reduce_fusion.319 = (f32[8,32]{1,0:T(8,128)S(1)}, f32[8,32]{1,0:T(8,128)S(1)}, f32[8,32]{1,0:T(8,128)S(1)}, f32[8,32]{1,0:T(8,128)S(1)}, f32[8,32]{1,0:T(...) fusion(f32[8,32,2,81]{3,1,2,0:T(8,128)S(1)} %bitcast.98), kind=kLoop, calls=%fused_computation.354 | loop fusion | bytes 38912 | tf_op jit(solution)/shard_map/slice | solution.py:47
  15.0 1.4 %slice_reduce_fusion.320 = (f32[8,32]{1,0:T(8,128)S(1)}, f32[8,32]{1,0:T(8,128)S(1)}, f32[8,32]{1,0:T(8,128)S(1)}, f32[8,32]{1,0:T(8,128)S(1)}, f32[8,32]{1,0:T(...) fusion(f32[8,32,2,81]{3,1,2,0:T(8,128)S(1)} %bitcast.99), kind=kLoop, calls=%fused_computation.355 | loop fusion | bytes 38912 | tf_op jit(solution)/shard_map/slice | solution.py:47
  16.4 1.4 %slice_reduce_fusion.321 = (f32[8,32]{1,0:T(8,128)S(1)}, f32[8,32]{1,0:T(8,128)S(1)}, f32[8,32]{1,0:T(8,128)S(1)}, f32[8,32]{1,0:T(8,128)S(1)}, f32[8,32]{1,0:T(...) fusion(f32[8,32,2,81]{3,1,2,0:T(8,128)S(1)} %bitcast.100), kind=kLoop, calls=%fused_computation.356 | loop fusion | bytes 38912 | tf_op jit(solution)/shard_map/slice | solution.py:47
  17.7 1.4 %slice_reduce_fusion.322 = (f32[8,32]{1,0:T(8,128)S(1)}, f32[8,32]{1,0:T(8,128)S(1)}, f32[8,32]{1,0:T(8,128)S(1)}, f32[8,32]{1,0:T(8,128)S(1)}, f32[8,32]{1,0:T(...) fusion(f32[8,32,2,81]{3,1,2,0:T(8,128)S(1)} %bitcast.101), kind=kLoop, calls=%fused_computation.357 | loop fusion | bytes 38912 | tf_op jit(solution)/shard_map/slice | solution.py:47
  21.9 1.5 %slice_reduce_fusion.33 = (f32[8,32]{1,0:T(8,128)S(1)}, f32[8,32]{1,0:T(8,128)S(1)}, f32[8,32]{1,0:T(8,128)S(1)}, f32[8,32]{1,0:T(8,128)S(1)}, f32[8,32]{1,0:T(8...) fusion(f32[8,32,2,81]{3,1,2,0:T(8,128)S(1)} %bitcast.86), kind=kLoop, calls=%fused_computation.66 | loop fusion | bytes 38912 | tf_op jit(solution)/shard_map/slice | solution.py:48
  23.4 1.4 %slice_reduce_fusion.156 = (f32[8,32]{1,0:T(8,128)S(1)}, f32[8,32]{1,0:T(8,128)S(1)}, f32[8,32]{1,0:T(8,128)S(1)}, f32[8,32]{1,0:T(8,128)S(1)}, f32[8,32]{1,0:T(...) fusion(f32[8,32,2,81]{3,1,2,0:T(8,128)S(1)} %bitcast.87), kind=kLoop, calls=%fused_computation.189 | loop fusion | bytes 38912 | tf_op jit(solution)/shard_map/slice | solution.py:47
  24.8 1.4 %slice_reduce_fusion.157 = (f32[8,32]{1,0:T(8,128)S(1)}, f32[8,32]{1,0:T(8,128)S(1)}, f32[8,32]{1,0:T(8,128)S(1)}, f32[8,32]{1,0:T(8,128)S(1)}, f32[8,32]{1,0:T(...) fusion(f32[8,32,2,81]{3,1,2,0:T(8,128)S(1)} %bitcast.88), kind=kLoop, calls=%fused_computation.190 | loop fusion | bytes 38912 | tf_op jit(solution)/shard_map/slice | solution.py:47
  26.2 1.4 %slice_reduce_fusion.158 = (f32[8,32]{1,0:T(8,128)S(1)}, f32[8,32]{1,0:T(8,128)S(1)}, f32[8,32]{1,0:T(8,128)S(1)}, f32[8,32]{1,0:T(8,128)S(1)}, f32[8,32]{1,0:T(...) fusion(f32[8,32,2,81]{3,1,2,0:T(8,128)S(1)} %bitcast.89), kind=kLoop, calls=%fused_computation.191 | loop fusion | bytes 38912 | tf_op jit(solution)/shard_map/slice | solution.py:47
  27.6 1.4 %slice_reduce_fusion.159 = (f32[8,32]{1,0:T(8,128)S(1)}, f32[8,32]{1,0:T(8,128)S(1)}, f32[8,32]{1,0:T(8,128)S(1)}, f32[8,32]{1,0:T(8,128)S(1)}, f32[8,32]{1,0:T(...) fusion(f32[8,32,2,81]{3,1,2,0:T(8,128)S(1)} %bitcast.90), kind=kLoop, calls=%fused_computation.192 | loop fusion | bytes 38912 | tf_op jit(solution)/shard_map/slice | solution.py:47
  28.9 1.4 %slice_reduce_fusion.160 = (f32[8,32]{1,0:T(8,128)S(1)}, f32[8,32]{1,0:T(8,128)S(1)}, f32[8,32]{1,0:T(8,128)S(1)}, f32[8,32]{1,0:T(8,128)S(1)}, f32[8,32]{1,0:T(...) fusion(f32[8,32,2,81]{3,1,2,0:T(8,128)S(1)} %bitcast.91), kind=kLoop, calls=%fused_computation.193 | loop fusion | bytes 38912 | tf_op jit(solution)/shard_map/slice | solution.py:47
  32.7 13.6 %all_gather.13 = f32[4,32,256]{2,1,0:T(8,128)S(1)} all-gather(f32[1,32,256]{2,1,0:T(8,128)S(1)} %slice_add_fusion.4), channel_id=1, replica_groups=mesh['patch'=2,'exp'=4,'strip'=2,'band'=2] {'exp'}, dimensions={0}, use_global_device_ids=true | all-gather | bytes 163840 | tf_op jit(solution)/shard_map/all_gather | solution.py:31
  49.8 2.0 %collective-permute-done.3 = f32[8,40,4]{2,1,0:T(8,128)S(1)} collective-permute-done((f32[8,40,4]{2,1,0:T(8,128)S(1)}, f32[8,40,4]{2,1,0:T(8,128)S(1)}, u32[]{:S(2)}, u32[]{:S(2)}) %collective-permute-start.3) | collective-permute-done | bytes 5152 | tf_op jit(solution)/shard_map/ppermute | solution.py:23
  52.0 11.3 %broadcast_select_fusion = (f32[8,32,256]{2,1,0:T(8,128)S(1)}, f32[8,32,256]{2,1,0:T(8,128)S(1)}, pred[8,32,256]{2,1,0:T(8,128)(4,1)S(1)}) fusion(f32[8,32]{1,0:T(8,128)S(1)} %get-tuple-element.347, f32[8,32]{1,0:T(8,128)S(1)} %get-tuple-element.348, f32[8,32]{1,0:T(8,128)S(1)} %get-tuple-element.349, f32[8,32]{1,0:T(8,128)S(1)} %get-tuple-element.350, ...), kind=kLoop, calls=%fused_computation.361 | loop fusion | flops 21692416 | bytes 21237760 | tf_op jit(solution)/shard_map/jit(_where)/select_n | solution.py:128
  63.5 14.8 %all_gather.15 = f32[4,3,32,256]{3,2,1,0:T(8,128)S(1)} all-gather(f32[1,3,32,256]{3,2,1,0:T(8,128)S(1)} %pad_maximum_fusion.6), channel_id=1, replica_groups=mesh['patch'=2,'exp'=4,'strip'=2,'band'=2] {'exp'}, dimensions={0}, use_global_device_ids=true | all-gather | bytes 491520 | tf_op jit(solution)/shard_map/all_gather | solution.py:31
  79.1 13.7 %all_gather.12 = f32[4,32,256]{2,1,0:T(8,128)S(1)} all-gather(f32[1,32,256]{2,1,0:T(8,128)S(1)} %slice_add_fusion.5), channel_id=1, replica_groups=mesh['patch'=2,'exp'=4,'strip'=2,'band'=2] {'exp'}, dimensions={0}, use_global_device_ids=true | all-gather | bytes 163840 | tf_op jit(solution)/shard_map/all_gather | solution.py:31
  93.6 15.3 %all_gather.14 = f32[4,3,32,256]{3,2,1,0:T(8,128)S(1)} all-gather(f32[1,3,32,256]{3,2,1,0:T(8,128)S(1)} %pad_maximum_fusion.5), channel_id=1, replica_groups=mesh['patch'=2,'exp'=4,'strip'=2,'band'=2] {'exp'}, dimensions={0}, use_global_device_ids=true | all-gather | bytes 491520 | tf_op jit(solution)/shard_map/all_gather | solution.py:31
  110.3 4.4 %collective-permute-start.4 = (f32[4,256]{1,0:T(4,128)S(1)}, f32[4,256]{1,0:T(4,128)S(1)}, u32[]{:S(2)}, u32[]{:S(2)}) collective-permute-start(f32[4,256]{1,0:T(4,128)S(1)} %get-tuple-element.526), channel_id=1, source_target_pairs={{0,2},{1,3},{4,6},{5,7},{8,10},{9,11},{12,14},{13,15},{16,18},{17,... | collective-permute-start | bytes 12296 | tf_op jit(solution)/shard_map/ppermute | solution.py:21
  114.7 1.5 %collective-permute-start.5 = (f32[4,256]{1,0:T(4,128)S(1)}, f32[4,256]{1,0:T(4,128)S(1)}, u32[]{:S(2)}, u32[]{:S(2)}) collective-permute-start(f32[4,256]{1,0:T(4,128)S(1)} %get-tuple-element.527), channel_id=1, source_target_pairs={{2,0},{3,1},{6,4},{7,5},{10,8},{11,9},{14,12},{15,13},{18,16},{19,... | collective-permute-start | bytes 12296 | tf_op jit(solution)/shard_map/ppermute | solution.py:23
  117.3 2.9 %collective-permute-done.5 = f32[4,256]{1,0:T(4,128)S(1)} collective-permute-done((f32[4,256]{1,0:T(4,128)S(1)}, f32[4,256]{1,0:T(4,128)S(1)}, u32[]{:S(2)}, u32[]{:S(2)}) %collective-permute-start.5) | collective-permute-done | bytes 4128 | tf_op jit(solution)/shard_map/ppermute | solution.py:23
  123.0 1.7 %collective-permute-done.7 = f32[40,4]{1,0:T(8,128)S(1)} collective-permute-done((f32[40,4]{1,0:T(8,128)S(1)}, f32[40,4]{1,0:T(8,128)S(1)}, u32[]{:S(2)}, u32[]{:S(2)}) %collective-permute-start.7) | collective-permute-done | bytes 672 | tf_op jit(solution)/shard_map/ppermute | solution.py:23
  125.6 9.2 %add_subtract_fusion = f32[8,32,256]{2,1,0:T(8,128)} fusion(f32[8,32,256]{2,1,0:T(8,128)S(1)} %copy-done, f32[8,32]{1,0:T(8,128)S(1)} %get-tuple-element.185, f32[8,32]{1,0:T(8,128)S(1)} %get-tuple-element.186, f32[8,32]{1,0:T(8,128)S(1)} %get-tuple-element.187, f32[8,32]{1,0:T(8,128)S(1)} %get-tuple-element.188, f32[8,32]{1,0:T(8,128)S(1)} %get-tuple-element.189, ...), kind=kLoop, calls=%fused_computation.31 | loop fusion | flops 21364736 | bytes 3346432 | tf_op jit(solution)/shard_map/sub | solution.py:136
  (98 shorter events, 21.8 us)
Async XLA Ops:
  0.6 7.1 %copy-start.6 = (f32[16,81]{1,0:T(8,128)S(1)}, f32[16,81]{1,0:T(8,128)}, u32[]{:S(2)}) copy-start(f32[16,81]{1,0:T(8,128)} %param.11) | copy-start | bytes 15556
  1.5 45.5 %collective-permute-start = (f32[8,4,256]{2,1,0:T(4,128)S(1)}, f32[8,4,256]{2,1,0:T(4,128)S(1)}, u32[]{:S(2)}, u32[]{:S(2)}) collective-permute-start(f32[8,4,256]{2,1,0:T(4,128)S(1)} %get-tuple-element.428), channel_id=1, source_target_pairs={{0,2},{1,3},{4,6},{5,7},{8,10},{9,11},{12,14},{13,15},{16,18},{17,... | collective-permute-start | bytes 98312 | tf_op jit(solution)/shard_map/ppermute | solution.py:21
  6.4 40.6 %collective-permute-start.1 = (f32[8,4,256]{2,1,0:T(4,128)S(1)}, f32[8,4,256]{2,1,0:T(4,128)S(1)}, u32[]{:S(2)}, u32[]{:S(2)}) collective-permute-start(f32[8,4,256]{2,1,0:T(4,128)S(1)} %get-tuple-element.429), channel_id=1, source_target_pairs={{2,0},{3,1},{6,4},{7,5},{10,8},{11,9},{14,12},{15,13},{18,16},{19,... | collective-permute-start | bytes 98312 | tf_op jit(solution)/shard_map/ppermute | solution.py:23
  7.7 0.7 copy-start.7
  19.1 1.4 %copy-start.8 = (s32[8,2,2]{0,2,1:T(2,128)S(1)}, s32[8,2,2]{0,2,1:T(2,128)}, u32[]{:S(2)}) copy-start(s32[8,2,2]{0,2,1:T(2,128)} %param.10) | copy-start | bytes 388
  30.3 1.4 %copy-start = (f32[8,32,256]{2,1,0:T(8,128)S(1)}, f32[8,32,256]{2,1,0:T(8,128)}, u32[]{:S(2)}) copy-start(f32[8,32,256]{2,1,0:T(8,128)} %param.7) | copy-start | bytes 786436
  31.7 1.0 copy-start.2
  46.4 0.7 copy-start.4
  47.2 2.6 %collective-permute-start.2 = (f32[8,40,4]{2,1,0:T(8,128)S(1)}, f32[8,40,4]{2,1,0:T(8,128)S(1)}, u32[]{:S(2)}, u32[]{:S(2)}) collective-permute-start(f32[8,40,4]{2,1,0:T(8,128)S(1)} %get-tuple-element.416), channel_id=1, source_target_pairs={{0,1},{2,3},{4,5},{6,7},{8,9},{10,11},{12,13},{14,15},{16,17},{18,... | collective-permute-start | bytes 15368 | tf_op jit(solution)/shard_map/ppermute | solution.py:21
  48.5 3.3 %collective-permute-start.3 = (f32[8,40,4]{2,1,0:T(8,128)S(1)}, f32[8,40,4]{2,1,0:T(8,128)S(1)}, u32[]{:S(2)}, u32[]{:S(2)}) collective-permute-start(f32[8,40,4]{2,1,0:T(8,128)S(1)} %get-tuple-element.417), channel_id=1, source_target_pairs={{1,0},{3,2},{5,4},{7,6},{9,8},{11,10},{13,12},{15,14},{17,16},{19,... | collective-permute-start | bytes 15368 | tf_op jit(solution)/shard_map/ppermute | solution.py:23
  78.3 0.7 copy-start.1
  92.8 0.7 copy-start.5
  108.9 1.0 slice-start
  108.9 1.0 slice-start.1
  108.9 1.0 slice-start.2
  110.3 15.3 %copy-start.3 = (f32[32,256]{1,0:T(8,128)}, f32[32,256]{1,0:T(8,128)S(1)}, u32[]{:S(2)}) copy-start(f32[32,256]{1,0:T(8,128)S(1)} %fusion.19) | copy-start | bytes 98308
  110.3 7.0 %collective-permute-start.4 = (f32[4,256]{1,0:T(4,128)S(1)}, f32[4,256]{1,0:T(4,128)S(1)}, u32[]{:S(2)}, u32[]{:S(2)}) collective-permute-start(f32[4,256]{1,0:T(4,128)S(1)} %get-tuple-element.526), channel_id=1, source_target_pairs={{0,2},{1,3},{4,6},{5,7},{8,10},{9,11},{12,14},{13,15},{16,18},{17,... | collective-permute-start | bytes 12296 | tf_op jit(solution)/shard_map/ppermute | solution.py:21
  114.7 5.5 %collective-permute-start.5 = (f32[4,256]{1,0:T(4,128)S(1)}, f32[4,256]{1,0:T(4,128)S(1)}, u32[]{:S(2)}, u32[]{:S(2)}) collective-permute-start(f32[4,256]{1,0:T(4,128)S(1)} %get-tuple-element.527), channel_id=1, source_target_pairs={{2,0},{3,1},{6,4},{7,5},{10,8},{11,9},{14,12},{15,13},{18,16},{19,... | collective-permute-start | bytes 12296 | tf_op jit(solution)/shard_map/ppermute | solution.py:23
  120.3 2.6 %collective-permute-start.6 = (f32[40,4]{1,0:T(8,128)S(1)}, f32[40,4]{1,0:T(8,128)S(1)}, u32[]{:S(2)}, u32[]{:S(2)}) collective-permute-start(f32[40,4]{1,0:T(8,128)S(1)} %get-tuple-element.512), channel_id=1, source_target_pairs={{0,1},{2,3},{4,5},{6,7},{8,9},{10,11},{12,13},{14,15},{16,17},{18,... | collective-permute-start | bytes 1928 | tf_op jit(solution)/shard_map/ppermute | solution.py:21
  121.6 3.1 %collective-permute-start.7 = (f32[40,4]{1,0:T(8,128)S(1)}, f32[40,4]{1,0:T(8,128)S(1)}, u32[]{:S(2)}, u32[]{:S(2)}) collective-permute-start(f32[40,4]{1,0:T(8,128)S(1)} %get-tuple-element.513), channel_id=1, source_target_pairs={{1,0},{3,2},{5,4},{7,6},{9,8},{11,10},{13,12},{15,14},{17,16},{19,... | collective-permute-start | bytes 1928 | tf_op jit(solution)/shard_map/ppermute | solution.py:23
where the time goes:
time: 135 us
  blocking collectives  57.4 us (43%)
  local copies, waits for them, and re-layouts  30.3 us (22%)
  other arithmetic  21.6 us (16%)
  starting transfers between devices  17.2 us (13%)
  waiting for transfers between devices  6.63 us (5%)
    all_gather x4, blocking collectives, joined(): pieces = jax.tree.map(lambda part: lax.all_gather(part, axis), value)  57.4 us
    slice x14, local copies, waits for them, and re-layouts, vary_conv(): low_acc = low_acc + kernels[..., 0, tap_at][..., None] * window  18.6 us
    ppermute x4, starting transfers between devices, extended(): lax.ppermute(tail, axis, [(i, (i + 1) % count) for i in range(ends)])  11.9 us
    select_n x1, other arithmetic, on_device(): jnp.where(is_valid, warped, -sentinel)  11.3 us
    sub x1, other arithmetic, on_device(): return (coadd_image, images - matched)  9.24 us
    ppermute x4, waiting for transfers between devices, extended(): lax.ppermute(head, axis, [((i + 1) % count, i) for i in range(ends)])  6.62 us
    ppermute x4, starting transfers between devices, extended(): lax.ppermute(head, axis, [((i + 1) % count, i) for i in range(ends)])  5.39 us
    slice x4, local copies, waits for them, and re-layouts, vary_conv(): high_acc = high_acc + kernels[..., 1, tap_at][..., None] * window  5.15 us
  transfers between devices with their start and end apart: 8, of which 3 were waited for; matrix products, arithmetic and copies ran while one was open for 18% of the time, Pallas kernels for 0%

commit v1 on v0

v1 whole, which is shorter than its diff:
```python
import functools

import jax
import jax.numpy as jnp
from jax import lax
from jax.experimental import pallas as pl
from jax.experimental.pallas import tpu as pltpu
from jax.sharding import PartitionSpec as P

TILE_ROWS = 16
KERNEL = 9
RIM = KERNEL // 2
LANES = 128
SUB = 8
SENTINEL = 1e30
MESH = pl.DeviceIdType.MESH
BF = jnp.bfloat16
F32 = jnp.float32


def split(value):
    high = value.astype(BF)
    return high, (value - high.astype(F32)).astype(BF)


def dot(left, right):
    return jnp.dot(left, right, preferred_element_type=F32)


def kernel(
    n_exp, n_strip, n_band, chunks, depth,
    images, mask, basis, match, bank,
    coadd_out, diff_out,
    pad, cpad, stage, recv, own, w_high, w_low, conv,
    local_sem, halo_send, halo_recv, stat_send, stat_recv, co_send, co_recv,
):
    count, rows, cols = images.shape
    tiles = rows // TILE_ROWS
    span = TILE_ROWS + 2 * RIM
    n_bank = bank.shape[0]
    part = max(SUB, rows // n_exp)
    owners = rows // part
    per = count // chunks
    me = lax.axis_index("exp")
    strip = lax.axis_index("strip")
    band = lax.axis_index("band")

    def there(d_strip, d_band):
        ok = jnp.bool_(True)
        if d_strip:
            ok = ok & (strip + d_strip >= 0) & (strip + d_strip < n_strip)
        if d_band:
            ok = ok & (band + d_band >= 0) & (band + d_band < n_band)
        return ok

    steps_s = (0,) if n_strip == 1 else (0, -1, 1)
    steps_b = (0,) if n_band == 1 else (0, -1, 1)
    sides = [(a, b) for a in steps_s for b in steps_b]

    def target(d_strip, d_band, exp):
        return {"exp": exp, "strip": strip + d_strip, "band": band + d_band}

    loads = [
        pltpu.make_async_copy(
            images.at[pl.ds(c * per, per)],
            pad.at[pl.ds(c * per, per), pl.ds(SUB, rows), pl.ds(LANES, cols)],
            local_sem.at[c],
        )
        for c in range(chunks)
    ]
    for load in loads:
        load.start()
    barrier = pltpu.get_barrier_semaphore()

    def each_exp(body, first=0):
        if n_exp <= 8:
            for d in range(first, n_exp):
                body(d)
        else:
            lax.fori_loop(first, n_exp, lambda d, _: (body(d), 0)[1], 0)

    for a, b in sides:
        @pl.when(there(a, b))
        def _(a=a, b=b):
            def greet(d):
                pl.semaphore_signal(
                    barrier, inc=1,
                    device_id=target(a, b, lax.rem(me + d, n_exp)), device_id_type=MESH,
                )
            each_exp(greet, 1 if (a, b) == (0, 0) else 0)
    near_s = 1 + sum(there(a, 0).astype(jnp.int32) for a in steps_s if a)
    near_b = 1 + sum(there(0, b).astype(jnp.int32) for b in steps_b if b)

    def places(a, b, height):
        src_rows = {0: (0, rows), -1: (0, height), 1: (rows - height, height)}[a]
        dst_rows = {0: SUB, -1: SUB + rows, 1: SUB - height}[a]
        src_cols = {0: (0, cols), -1: (0, LANES), 1: (cols - LANES, LANES)}[b]
        dst_cols = {0: LANES, -1: LANES + cols, 1: 0}[b]
        return src_rows, dst_rows, src_cols, dst_cols

    def rim_copy(c, at, a, b):
        src_rows, dst_rows, src_cols, dst_cols = places(a, b, depth)
        return pltpu.make_async_remote_copy(
            src_ref=images.at[pl.ds(c * per, per), pl.ds(*src_rows), pl.ds(*src_cols)],
            dst_ref=pad.at[
                pl.ds(c * per, per), pl.ds(dst_rows, src_rows[1]), pl.ds(dst_cols, src_cols[1])
            ],
            send_sem=halo_send.at[c, at],
            recv_sem=halo_recv.at[c, at],
            device_id=target(a, b, me),
            device_id_type=MESH,
        )

    rims = [(at, a, b) for at, (a, b) in enumerate(sides) if (a, b) != (0, 0)]

    for a, b in sides:
        if (a, b) == (0, 0):
            continue

        @pl.when(jnp.logical_not(there(-a, -b)))
        def _(a=a, b=b):
            src_rows, dst_rows, src_cols, dst_cols = places(a, b, SUB)
            pad[:, dst_rows:dst_rows + src_rows[1], dst_cols:dst_cols + src_cols[1]] = jnp.zeros(
                (count, src_rows[1], src_cols[1]), F32
            )
            cpad[dst_rows:dst_rows + src_rows[1], dst_cols:dst_cols + src_cols[1]] = jnp.zeros(
                (src_rows[1], src_cols[1]), F32
            )
    if n_strip == 1:
        for start in (0, SUB + rows):
            pad[:, start:start + SUB, :] = jnp.zeros((count, SUB, cols + 2 * LANES), F32)
            cpad[start:start + SUB, :] = jnp.zeros((SUB, cols + 2 * LANES), F32)
    if n_band == 1:
        for start in (0, LANES + cols):
            pad[:, :, start:start + LANES] = jnp.zeros((count, rows + 2 * SUB, LANES), F32)
            cpad[:, start:start + LANES] = jnp.zeros((rows + 2 * SUB, LANES), F32)

    pl.semaphore_wait(barrier, near_s * near_b * n_exp - 1)
    for c in range(chunks):
        for at, a, b in rims:
            @pl.when(there(a, b))
            def _(c=c, at=at, a=a, b=b):
                rim_copy(c, at, a, b).start()

    taps = KERNEL * KERNEL
    wide = 2 * LANES
    weights = bank[...]
    normed = weights / jnp.sum(weights, axis=1, keepdims=True)
    tap = lax.broadcasted_iota(jnp.int32, (taps, wide), 0)
    col = lax.broadcasted_iota(jnp.int32, (taps, wide), 1)
    tap_row = jnp.zeros((taps, wide), jnp.int32)
    for i in range(1, KERNEL):
        tap_row = tap_row + (tap >= i * KERNEL).astype(jnp.int32)
    place = (tap - tap_row * KERNEL) * span + tap_row
    spread = jnp.where(col == place, 1.0, 0.0).astype(BF)
    part_a, rest = split(normed)
    part_b = rest
    part_c = (normed - part_a.astype(F32) - part_b.astype(F32)).astype(BF)
    base = dot(part_a, spread) + dot(part_b, spread) + dot(part_c, spread)
    y_at = lax.broadcasted_iota(jnp.int32, (TILE_ROWS, wide), 0)
    for k in range(n_bank):
        line = jnp.broadcast_to(base[k:k + 1, :], (TILE_ROWS, wide))
        for bit in range(4):
            moved = pltpu.roll(line, 1 << bit, 1)
            line = jnp.where((y_at & (1 << bit)) != 0, moved, line)
        high, low = split(line)
        w_high[k] = high
        w_low[k] = low

    lane = lax.broadcasted_iota(jnp.int32, (TILE_ROWS, cols), 1)
    blend = (band * cols + lane).astype(F32) / (cols * n_band - 1)

    def shifted(field):
        total = cols + 2 * LANES
        moved = []
        for j in range(KERNEL):
            turn = (RIM - j) % total
            whole = field if turn == 0 else pltpu.roll(field, turn, 1)
            moved.append(whole[:, LANES:LANES + cols])
        pieces = []
        fill = jnp.zeros((wide - KERNEL * span, cols), F32)
        for t in range(tiles):
            at = t * TILE_ROWS
            stack = jnp.concatenate([m[at:at + span] for m in moved] + [fill], axis=0)
            pieces.append(split(stack))
        return pieces

    def stat_copy(c, who):
        return pltpu.make_async_remote_copy(
            src_ref=stage.at[pl.ds(c * per, per), pl.ds(pl.multiple_of(who * part, part), part)],
            dst_ref=recv.at[me, pl.ds(c * per, per)],
            send_sem=stat_send.at[c, who],
            recv_sem=stat_recv.at[c, me],
            device_id=target(0, 0, who),
            device_id_type=MESH,
        )

    def stat_arrival(c, who):
        return pltpu.make_async_remote_copy(
            src_ref=stage.at[pl.ds(c * per, per), pl.ds(0, part)],
            dst_ref=recv.at[who, pl.ds(c * per, per)],
            send_sem=stat_send.at[c, 0],
            recv_sem=stat_recv.at[c, who],
            device_id=target(0, 0, who),
            device_id_type=MESH,
        )

    def warp(e, _):
        pieces = shifted(pad[e, SUB - RIM:SUB + rows + RIM, :])
        for t in range(tiles):
            s_high, s_low = pieces[t]
            first, second = basis[e, t, 0], basis[e, t, 1]
            high = jnp.concatenate([w_high[first], w_high[second]], axis=0)
            low = jnp.concatenate([w_low[first], w_low[second]], axis=0)
            got = dot(high, s_high) + dot(low, s_high) + dot(high, s_low)
            value = (1.0 - blend) * got[:TILE_ROWS] + blend * got[TILE_ROWS:]
            here = pl.ds(t * TILE_ROWS, TILE_ROWS)
            stage[e, here, :] = jnp.where(mask[e, here, :] == 1, value, SENTINEL)
        return 0

    def others(body):
        def one(d):
            who = lax.rem(me + d, n_exp)
            if owners == n_exp:
                body(who)
            else:
                @pl.when(who < owners)
                def _():
                    body(who)
        each_exp(one, 1)

    for c in range(chunks):
        loads[c].wait()
        for at, a, b in rims:
            @pl.when(there(-a, -b))
            def _(c=c, at=at, a=a, b=b):
                rim_copy(c, at, a, b).wait_recv()
        lax.fori_loop(c * per, (c + 1) * per, warp, 0)
        others(lambda who, c=c: stat_copy(c, who).start())

    def insert(state, value):
        total, number, l0, l1, l2, h0, h1, h2 = state
        valid = value < 0.5 * SENTINEL
        total = total + jnp.where(valid, value, 0.0)
        number = number + jnp.where(valid, 1.0, 0.0)
        x = value
        l0, x = jnp.minimum(l0, x), jnp.maximum(l0, x)
        l1, x = jnp.minimum(l1, x), jnp.maximum(l1, x)
        l2 = jnp.minimum(l2, x)
        x = jnp.where(valid, value, -SENTINEL)
        h0, x = jnp.maximum(h0, x), jnp.minimum(h0, x)
        h1, x = jnp.maximum(h1, x), jnp.minimum(h1, x)
        h2 = jnp.maximum(h2, x)
        return total, number, l0, l1, l2, h0, h1, h2

    def co_places(a, b):
        rows_from = 0
        src_cols = {0: (0, cols), -1: (0, LANES), 1: (cols - LANES, LANES)}[b]
        dst_cols = {0: LANES, -1: LANES + cols, 1: 0}[b]
        return src_cols, dst_cols

    def co_copy(at, a, b, source, exp):
        src_cols, dst_cols = co_places(a, b)
        if a == 0:
            src_row, height = 0, part
            dst_row = pl.multiple_of(SUB + source * part, SUB)
        elif a == -1:
            src_row, height, dst_row = 0, SUB, SUB + rows
        else:
            src_row, height, dst_row = part - SUB, SUB, 0
        slot = source if a == 0 else 0
        return pltpu.make_async_remote_copy(
            src_ref=own.at[pl.ds(src_row, height), pl.ds(*src_cols)],
            dst_ref=cpad.at[pl.ds(dst_row, height), pl.ds(dst_cols, src_cols[1])],
            send_sem=co_send.at[at, exp],
            recv_sem=co_recv.at[at, slot],
            device_id=target(a, b, exp),
            device_id_type=MESH,
        )

    def sends(a):
        if a == 0:
            return jnp.bool_(True)
        return me == (0 if a == -1 else owners - 1)

    def each_send(act):
        for at, (a, b) in enumerate(sides):
            @pl.when(there(a, b) & sends(a))
            def _(at=at, a=a, b=b):
                def one(d):
                    act(co_copy(at, a, b, me, lax.rem(me + d, n_exp)))
                each_exp(one, 1 if (a, b) == (0, 0) else 0)

    def join():
        zero = jnp.zeros((part, cols), F32)
        top = jnp.full((part, cols), SENTINEL, F32)
        state = (zero, zero, top, top, top, -top, -top, -top)
        mine = pl.ds(pl.multiple_of(me * part, part), part)
        for e in range(count):
            state = insert(state, stage[e, mine, :])

        def take(d, state):
            who = lax.rem(me + d, n_exp)
            for c in range(chunks):
                stat_arrival(c, who).wait_recv()
                for e in range(c * per, (c + 1) * per):
                    state = insert(state, recv[who, e])
            return state

        state = lax.fori_loop(1, n_exp, take, state)
        total, number, l0, l1, l2, h0, h1, h2 = state
        value = (total - (l0 + l1 + l2) - (h0 + h1 + h2)) / (number - 6.0)
        own[...] = value
        cpad[pl.ds(pl.multiple_of(SUB + me * part, SUB), part), LANES:LANES + cols] = value
        each_send(lambda copy: copy.start())

    if owners == n_exp:
        join()
    else:
        pl.when(me < owners)(join)

    for at, (a, b) in enumerate(sides):
        @pl.when(there(-a, -b))
        def _(at=at, a=a, b=b):
            if a == 0:
                if b == 0:
                    others(lambda who: co_copy(at, a, b, who, me).wait_recv())
                else:
                    for who in range(owners):
                        co_copy(at, a, b, who, me).wait_recv()
            else:
                co_copy(at, a, b, 0, me).wait_recv()

    pieces = shifted(cpad[SUB - RIM:SUB + rows + RIM, :])
    high = w_high[...].reshape(n_bank * TILE_ROWS, wide)
    low = w_low[...].reshape(n_bank * TILE_ROWS, wide)
    for t in range(tiles):
        s_high, s_low = pieces[t]
        got = dot(high, s_high) + dot(low, s_high) + dot(high, s_low)
        conv[t * n_bank:(t + 1) * n_bank] = got.reshape(n_bank, TILE_ROWS, cols)
    coadd_out[...] = cpad[SUB:SUB + rows, LANES:LANES + cols]

    def final(e, _):
        for t in range(tiles):
            first, second = match[e, t, 0], match[e, t, 1]
            one, two = conv[t * n_bank + first], conv[t * n_bank + second]
            value = (1.0 - blend) * one + blend * two
            here = pl.ds(t * TILE_ROWS, TILE_ROWS)
            source = pad[e, SUB + t * TILE_ROWS:SUB + (t + 1) * TILE_ROWS, LANES:LANES + cols]
            diff_out[e, here, :] = source - value
        return 0

    lax.fori_loop(0, count, final, 0)

    for c in range(chunks):
        for at, a, b in rims:
            @pl.when(there(a, b))
            def _(c=c, at=at, a=a, b=b):
                rim_copy(c, at, a, b).wait_send()
        others(lambda who, c=c: stat_copy(c, who).wait_send())
    if owners == n_exp:
        each_send(lambda copy: copy.wait_send())
    else:
        pl.when(me < owners)(lambda: each_send(lambda copy: copy.wait_send()))


def on_device(sizes, images, valid_mask, basis_index, match_index, psf_bank):
    n_exp, n_strip, n_band = sizes
    count, rows, cols = images.shape
    chunks = 2 if count % 2 == 0 else 1
    part = max(SUB, rows // n_exp)
    owners = rows // part
    n_sides = (1 if n_strip == 1 else 3) * (1 if n_band == 1 else 3)
    tiles = rows // TILE_ROWS
    n_bank = psf_bank.shape[0]
    vmem = pl.BlockSpec(memory_space=pltpu.VMEM)
    smem = pl.BlockSpec(memory_space=pltpu.SMEM)
    dma = pltpu.SemaphoreType.DMA
    return pl.pallas_call(
        functools.partial(kernel, n_exp, n_strip, n_band, chunks, DEPTH),
        out_shape=(
            jax.ShapeDtypeStruct((rows, cols), F32),
            jax.ShapeDtypeStruct(images.shape, F32),
        ),
        in_specs=[pl.BlockSpec(memory_space=pl.ANY), vmem, smem, smem, vmem],
        out_specs=(vmem, vmem),
        scratch_shapes=[
            pltpu.VMEM((count, rows + 2 * SUB, cols + 2 * LANES), F32),
            pltpu.VMEM((rows + 2 * SUB, cols + 2 * LANES), F32),
            pltpu.VMEM((count, rows, cols), F32),
            pltpu.VMEM((n_exp, count, part, cols), F32),
            pltpu.VMEM((part, cols), F32),
            pltpu.VMEM((n_bank, TILE_ROWS, 2 * LANES), BF),
            pltpu.VMEM((n_bank, TILE_ROWS, 2 * LANES), BF),
            pltpu.VMEM((tiles * n_bank, TILE_ROWS, cols), F32),
            dma((chunks,)),
            dma((chunks, n_sides)),
            dma((chunks, n_sides)),
            dma((chunks, n_exp)),
            dma((chunks, n_exp)),
            dma((n_sides, n_exp)),
            dma((n_sides, owners)),
        ],
        compiler_params=pltpu.CompilerParams(
            collective_id=0, has_side_effects=True, vmem_limit_bytes=48 * 1024 * 1024
        ),
    )(images, valid_mask, basis_index, match_index, psf_bank)


DEPTH = RIM


def solution(mesh):
    sizes = tuple(mesh.shape[name] for name in ("exp", "strip", "band"))
    return jax.shard_map(
        functools.partial(on_device, sizes),
        mesh=mesh,
        in_specs=(
            P(("patch", "exp"), "strip", "band"),
            P(("patch", "exp"), "strip", "band"),
            P(("patch", "exp"), "strip", None),
            P(("patch", "exp"), "strip", None),
            P(),
        ),
        out_specs=(P(("patch", "strip"), "band"), P(("patch", "exp"), "strip", "band")),
        check_vma=False,
    )
```

time: 135 us -> 28.8 us (0.21)
  blocking collectives: 57.4 us -> 0 us
  local copies, waits for them, and re-layouts: 30.3 us -> 4.1 us
  Pallas kernels: 0 us -> 23.9 us
  other arithmetic: 21.6 us -> 0 us
  starting transfers between devices: 17.2 us -> 0 us
  waiting for transfers between devices: 6.63 us -> 0 us
    all_gather x4 -> x0, blocking collectives: 57.4 us -> none  [joined(): pieces = jax.tree.map(lambda part: lax.all_gather(part, axis), value)]
    slice x33 -> x0, local copies, waits for them, and re-layouts: 26.6 us -> none  [the longest x14 18.6 us: vary_conv(): low_acc = low_acc + kernels[..., 0, tap_at][..., None] * window]
    pallas_call x0 -> x1, Pallas kernels: none -> 23.9 us  [on_device(): pl.pallas_call(functools.partial(kernel, n_exp, n_strip, n_band, chunks,...]
    ppermute x8 -> x0, starting transfers between devices: 17.2 us -> none  [the longest x4 11.9 us: extended(): lax.ppermute(tail, axis, [(i, (i + 1) % count) for i in range(ends)])]
    select_n x2 -> x0, other arithmetic: 11.4 us -> none  [the longest x1 11.3 us: on_device(): jnp.where(is_valid, warped, -sentinel)]
    sub x1 -> x0, other arithmetic: 9.24 us -> none  [on_device(): return (coadd_image, images - matched)]
    ppermute x8 -> x0, waiting for transfers between devices: 6.63 us -> none  [the longest x4 6.62 us: extended(): lax.ppermute(head, axis, [((i + 1) % count, i) for i in range(ends)])]
    unnamed x19 -> x12, local copies, waits for them, and re-layouts: 3.54 us -> 4.1 us
  transfers between devices with their start and end apart: 8 -> 0, of which waited for: 3 -> 0; matrix products, arithmetic and copies ran while one was open for 18% -> 0% of each run, Pallas kernels for 0% -> 0%
where the time goes in v1:
time: 28.8 us; the launch traced here: 28.6 us
  Pallas kernels  23.9 us (83%)
  local copies, waits for them, and re-layouts  4.1 us (14%)
  between operations  0.66 us (2%)
    pallas_call x1, Pallas kernels, on_device(): pl.pallas_call(functools.partial(kernel, n_exp, n_strip, n_band, chunks,...  23.9 us
    unnamed x12, local copies, waits for them, and re-layouts  4.1 us

profile of v1, /device:TPU:0, one launch (start us, length us, event | category | flops | bytes accessed | tf_op | source)
XLA Modules:
  0.0 28.6 jit_solution(4633039750788313246)
XLA Ops:
  0.6 0.0 copy-start.2
  0.6 0.0 copy-start.3
  0.7 0.8 %copy.7.basis = s32[8,2,2]{2,1,0:T(2,128)S(1)} copy(s32[8,2,2]{0,2,1:T(2,128)} %param.7) | data formatting | bytes 256 | tf_op args[2]
  1.4 0.0 copy-done.3
  1.4 0.1 copy.8.match
  1.5 0.0 copy-done.2
  1.5 0.0 copy-start
  1.5 0.9 %copy-done = f32[8,32,256]{2,1,0:T(8,128)S(1)} copy-done((f32[8,32,256]{2,1,0:T(8,128)S(1)}, f32[8,32,256]{2,1,0:T(8,128)}, u32[]{:S(2)}) %copy-start) | copy-done | bytes 262168
  2.5 0.0 copy-start.1
  2.5 0.9 %copy-done.1 = s32[8,32,256]{2,1,0:T(8,128)S(1)} copy-done((s32[8,32,256]{2,1,0:T(8,128)S(1)}, s32[8,32,256]{2,1,0:T(8,128)}, u32[]{:S(2)}) %copy-start.1) | copy-done | bytes 262168
  3.4 23.9 %shard_map.68 = (f32[32,256]{1,0:T(8,128)S(1)}, f32[8,32,256]{2,1,0:T(8,128)S(1)}) custom-call(f32[8,32,256]{2,1,0:T(8,128)S(1)} %copy-done, s32[8,32,256]{2,1,0:T(8,128)S(1)} %copy-done.1, s32[8,2,2]{2,1,0:T(2,128)S(1)} %copy.7.basis, s32[8,2,2]{2,1,0:T(2,128)S(1)} %copy.8.match, f32[16,81]{1,0:T(8,128)S(1)} %copy-done.2), custom_call_target="tpu_custom_call" | custom-call | tf_op jit(solution)/shard_map/pallas_call | solution.py:379
  27.3 0.6 %copy.11 = f32[32,256]{1,0:T(8,128)} copy(f32[32,256]{1,0:T(8,128)S(1)} %get-tuple-element.4) | data formatting | bytes 65536
  27.9 0.7 %copy.12 = f32[8,32,256]{2,1,0:T(8,128)} copy(f32[8,32,256]{2,1,0:T(8,128)S(1)} %get-tuple-element.5) | data formatting | bytes 524288
Async XLA Ops:
  0.6 0.9 %copy-start.2 = (f32[16,81]{1,0:T(8,128)S(1)}, f32[16,81]{1,0:T(8,128)}, u32[]{:S(2)}) copy-start(f32[16,81]{1,0:T(8,128)} %bank.1) | copy-start | bytes 15556
  0.6 0.8 %copy-start.3 = (s32[8,2,2]{0,2,1:T(2,128)S(1)}, s32[8,2,2]{0,2,1:T(2,128)}, u32[]{:S(2)}) copy-start(s32[8,2,2]{0,2,1:T(2,128)} %param.8) | copy-start | bytes 388
  1.5 1.0 %copy-start = (f32[8,32,256]{2,1,0:T(8,128)S(1)}, f32[8,32,256]{2,1,0:T(8,128)}, u32[]{:S(2)}) copy-start(f32[8,32,256]{2,1,0:T(8,128)} %images.1) | copy-start | bytes 786436
  2.5 0.9 %copy-start.1 = (s32[8,32,256]{2,1,0:T(8,128)S(1)}, s32[8,32,256]{2,1,0:T(8,128)}, u32[]{:S(2)}) copy-start(s32[8,32,256]{2,1,0:T(8,128)} %mask.1) | copy-start | bytes 786436

commit v2 on v1

--- a/solution.py
+++ b/solution.py
@@ -29,15 +29,16 @@
 
 def kernel(
     n_exp, n_strip, n_band, chunks, depth,
-    images, mask, basis, match, bank,
+    images, mask_in, basis_in, match_in, bank_in,
     coadd_out, diff_out,
+    mask, basis, match, bank,
     pad, cpad, stage, recv, own, w_high, w_low, conv,
-    local_sem, halo_send, halo_recv, stat_send, stat_recv, co_send, co_recv,
+    local_sem, in_sem, halo_send, halo_recv, stat_send, stat_recv, co_send, co_recv,
 ):
     count, rows, cols = images.shape
     tiles = rows // TILE_ROWS
     span = TILE_ROWS + 2 * RIM
-    n_bank = bank.shape[0]
+    n_bank = bank_in.shape[0]
     part = max(SUB, rows // n_exp)
     owners = rows // part
     per = count // chunks
@@ -60,16 +61,6 @@
     def target(d_strip, d_band, exp):
         return {"exp": exp, "strip": strip + d_strip, "band": band + d_band}
 
-    loads = [
-        pltpu.make_async_copy(
-            images.at[pl.ds(c * per, per)],
-            pad.at[pl.ds(c * per, per), pl.ds(SUB, rows), pl.ds(LANES, cols)],
-            local_sem.at[c],
-        )
-        for c in range(chunks)
-    ]
-    for load in loads:
-        load.start()
     barrier = pltpu.get_barrier_semaphore()
 
     def each_exp(body, first=0):
@@ -88,6 +79,21 @@
                     device_id=target(a, b, lax.rem(me + d, n_exp)), device_id_type=MESH,
                 )
             each_exp(greet, 1 if (a, b) == (0, 0) else 0)
+    loads = [
+        pltpu.make_async_copy(
+            images.at[pl.ds(c * per, per)],
+            pad.at[pl.ds(c * per, per), pl.ds(SUB, rows), pl.ds(LANES, cols)],
+            local_sem.at[c],
+        )
+        for c in range(chunks)
+    ]
+    bank_load = pltpu.make_async_copy(bank_in, bank, in_sem.at[0])
+    mask_load = pltpu.make_async_copy(mask_in, mask, in_sem.at[1])
+    basis_load = pltpu.make_async_copy(basis_in, basis, in_sem.at[2])
+    match_load = pltpu.make_async_copy(match_in, match, in_sem.at[3])
+    for load in [bank_load] + loads + [mask_load, basis_load, match_load]:
+        load.start()
+
     near_s = 1 + sum(there(a, 0).astype(jnp.int32) for a in steps_s if a)
     near_b = 1 + sum(there(0, b).astype(jnp.int32) for b in steps_b if b)
 
@@ -101,7 +107,11 @@
     def rim_copy(c, at, a, b):
         src_rows, dst_rows, src_cols, dst_cols = places(a, b, depth)
         return pltpu.make_async_remote_copy(
-            src_ref=images.at[pl.ds(c * per, per), pl.ds(*src_rows), pl.ds(*src_cols)],
+            src_ref=pad.at[
+                pl.ds(c * per, per),
+                pl.ds(SUB + src_rows[0], src_rows[1]),
+                pl.ds(LANES + src_cols[0], src_cols[1]),
+            ],
             dst_ref=pad.at[
                 pl.ds(c * per, per), pl.ds(dst_rows, src_rows[1]), pl.ds(dst_cols, src_cols[1])
             ],
@@ -135,15 +145,9 @@
             pad[:, :, start:start + LANES] = jnp.zeros((count, rows + 2 * SUB, LANES), F32)
             cpad[:, start:start + LANES] = jnp.zeros((rows + 2 * SUB, LANES), F32)
 
-    pl.semaphore_wait(barrier, near_s * near_b * n_exp - 1)
-    for c in range(chunks):
-        for at, a, b in rims:
-            @pl.when(there(a, b))
-            def _(c=c, at=at, a=a, b=b):
-                rim_copy(c, at, a, b).start()
-
     taps = KERNEL * KERNEL
     wide = 2 * LANES
+    bank_load.wait()
     weights = bank[...]
     normed = weights / jnp.sum(weights, axis=1, keepdims=True)
     tap = lax.broadcasted_iota(jnp.int32, (taps, wide), 0)
@@ -167,6 +171,14 @@
         w_high[k] = high
         w_low[k] = low
 
+    pl.semaphore_wait(barrier, near_s * near_b * n_exp - 1)
+    for c in range(chunks):
+        loads[c].wait()
+        for at, a, b in rims:
+            @pl.when(there(a, b))
+            def _(c=c, at=at, a=a, b=b):
+                rim_copy(c, at, a, b).start()
+
     lane = lax.broadcasted_iota(jnp.int32, (TILE_ROWS, cols), 1)
     blend = (band * cols + lane).astype(F32) / (cols * n_band - 1)
 
@@ -209,7 +221,7 @@
         pieces = shifted(pad[e, SUB - RIM:SUB + rows + RIM, :])
         for t in range(tiles):
             s_high, s_low = pieces[t]
-            first, second = basis[e, t, 0], basis[e, t, 1]
+            first, second = basis[t, 0, e], basis[t, 1, e]
             high = jnp.concatenate([w_high[first], w_high[second]], axis=0)
             low = jnp.concatenate([w_low[first], w_low[second]], axis=0)
             got = dot(high, s_high) + dot(low, s_high) + dot(high, s_low)
@@ -229,8 +241,9 @@
                     body(who)
         each_exp(one, 1)
 
+    mask_load.wait()
+    basis_load.wait()
     for c in range(chunks):
-        loads[c].wait()
         for at, a, b in rims:
             @pl.when(there(-a, -b))
             def _(c=c, at=at, a=a, b=b):
@@ -340,9 +353,11 @@
         conv[t * n_bank:(t + 1) * n_bank] = got.reshape(n_bank, TILE_ROWS, cols)
     coadd_out[...] = cpad[SUB:SUB + rows, LANES:LANES + cols]
 
+    match_load.wait()
+
     def final(e, _):
         for t in range(tiles):
-            first, second = match[e, t, 0], match[e, t, 1]
+            first, second = match[t, 0, e], match[t, 1, e]
             one, two = conv[t * n_bank + first], conv[t * n_bank + second]
             value = (1.0 - blend) * one + blend * two
             here = pl.ds(t * TILE_ROWS, TILE_ROWS)
@@ -364,6 +379,20 @@
         pl.when(me < owners)(lambda: each_send(lambda copy: copy.wait_send()))
 
 
+def deliver(count, coadd, diff, coadd_out, diff_out, sem):
+    half = max(count // 2, 1)
+    copies = [
+        pltpu.make_async_copy(coadd, coadd_out, sem.at[0]),
+        pltpu.make_async_copy(diff.at[:half], diff_out.at[:half], sem.at[1]),
+    ]
+    if count > half:
+        copies.append(pltpu.make_async_copy(diff.at[half:], diff_out.at[half:], sem.at[2]))
+    for copy in copies:
+        copy.start()
+    for copy in copies:
+        copy.wait()
+
+
 def on_device(sizes, images, valid_mask, basis_index, match_index, psf_bank):
     n_exp, n_strip, n_band = sizes
     count, rows, cols = images.shape
@@ -374,17 +403,20 @@
     tiles = rows // TILE_ROWS
     n_bank = psf_bank.shape[0]
     vmem = pl.BlockSpec(memory_space=pltpu.VMEM)
-    smem = pl.BlockSpec(memory_space=pltpu.SMEM)
     dma = pltpu.SemaphoreType.DMA
-    return pl.pallas_call(
+    results = pl.pallas_call(
         functools.partial(kernel, n_exp, n_strip, n_band, chunks, DEPTH),
         out_shape=(
-            jax.ShapeDtypeStruct((rows, cols), F32),
-            jax.ShapeDtypeStruct(images.shape, F32),
+            OUT_TYPE((rows, cols), F32),
+            OUT_TYPE(images.shape, F32),
         ),
-        in_specs=[pl.BlockSpec(memory_space=pl.ANY), vmem, smem, smem, vmem],
+        in_specs=[pl.BlockSpec(memory_space=pltpu.HBM)] * 5,
         out_specs=(vmem, vmem),
         scratch_shapes=[
+            pltpu.VMEM(valid_mask.shape, jnp.int32),
+            pltpu.SMEM((tiles, 2, count), jnp.int32),
+            pltpu.SMEM((tiles, 2, count), jnp.int32),
+            pltpu.VMEM(psf_bank.shape, F32),
             pltpu.VMEM((count, rows + 2 * SUB, cols + 2 * LANES), F32),
             pltpu.VMEM((rows + 2 * SUB, cols + 2 * LANES), F32),
             pltpu.VMEM((count, rows, cols), F32),
@@ -394,6 +426,7 @@
             pltpu.VMEM((n_bank, TILE_ROWS, 2 * LANES), BF),
             pltpu.VMEM((tiles * n_bank, TILE_ROWS, cols), F32),
             dma((chunks,)),
+            dma((4,)),
             dma((chunks, n_sides)),
             dma((chunks, n_sides)),
             dma((chunks, n_exp)),
@@ -402,12 +435,28 @@
             dma((n_sides, owners)),
         ],
         compiler_params=pltpu.CompilerParams(
-            collective_id=0, has_side_effects=True, vmem_limit_bytes=48 * 1024 * 1024
+            collective_id=0, has_side_effects=True, vmem_limit_bytes=LIMIT
         ),
-    )(images, valid_mask, basis_index, match_index, psf_bank)
+    )(
+        images, valid_mask, basis_index.transpose(1, 2, 0), match_index.transpose(1, 2, 0), psf_bank
+    )
+    return pl.pallas_call(
+        functools.partial(deliver, count),
+        out_shape=(
+            jax.ShapeDtypeStruct((rows, cols), F32),
+            jax.ShapeDtypeStruct(images.shape, F32),
+        ),
+        in_specs=[IN_SPEC, IN_SPEC],
+        out_specs=(pl.BlockSpec(memory_space=pltpu.HBM),) * 2,
+        scratch_shapes=[dma((3,))],
+        compiler_params=pltpu.CompilerParams(vmem_limit_bytes=1024 * 1024),
+    )(*results)
 
 
 DEPTH = RIM
+LIMIT = 62 * 1024 * 1024
+OUT_TYPE = pltpu.VMEM
+IN_SPEC = pl.BlockSpec(memory_space=pltpu.VMEM)
 
 
 def solution(mesh):

time: 28.8 us -> 24.7 us (0.86)
  local copies, waits for them, and re-layouts: 4.1 us -> 0 us
    unnamed x12 -> x0, local copies, waits for them, and re-layouts: 4.1 us -> none
    pallas_call x1, Pallas kernels: 23.9 us -> 23.1 us  [on_device(): pl.pallas_call(functools.partial(kernel, n_exp, n_strip, n_band, chunks,...]
    pallas_call x0 -> x1, Pallas kernels: none -> 0.74 us  [on_device(): pl.pallas_call(functools.partial(deliver, count), out_shape=(jax.ShapeDty...]
where the time goes in v2:
time: 24.7 us; the launch traced here: 24.5 us
  Pallas kernels  23.9 us (97%)
  between operations  0.64 us (3%)
    pallas_call x1, Pallas kernels, on_device(): pl.pallas_call(functools.partial(kernel, n_exp, n_strip, n_band, chunks,...  23.1 us
    pallas_call x1, Pallas kernels, on_device(): pl.pallas_call(functools.partial(deliver, count), out_shape=(jax.ShapeDty...  0.74 us

profile of v2, /device:TPU:0, one launch (start us, length us, event | category | flops | bytes accessed | tf_op | source)
XLA Modules:
  0.0 24.5 jit_solution(12618284749766759688)
XLA Ops:
  0.6 23.1 %shard_map.68 = (f32[32,256]{1,0:T(8,128)S(1)}, f32[8,32,256]{2,1,0:T(8,128)S(1)}) custom-call(f32[8,32,256]{2,1,0:T(8,128)} %images.1, s32[8,32,256]{2,1,0:T(8,128)} %mask_in.1, s32[2,2,8]{2,1,0:T(2,128)} %bitcast.2, s32[2,2,8]{2,1,0:T(2,128)} %bitcast.3, f32[16,81]{1,0:T(8,128)} %bank_in.1), custom_call_target="tpu_custom_call" | custom-call | tf_op jit(solution)/shard_map/pallas_call | solution.py:407
  23.8 0.7 %shard_map.69 = (f32[32,256]{1,0:T(8,128)}, f32[8,32,256]{2,1,0:T(8,128)}) custom-call(f32[32,256]{1,0:T(8,128)S(1)} %get-tuple-element.4.coadd, f32[8,32,256]{2,1,0:T(8,128)S(1)} %get-tuple-element.5.diff), custom_call_target="tpu_custom_call" | custom-call | tf_op jit(solution)/shard_map/pallas_call | solution.py:443

commit v3 on v2

--- a/solution.py
+++ b/solution.py
@@ -65,7 +65,7 @@
 
     def each_exp(body, first=0):
         if n_exp <= 8:
-            for d in range(first, n_exp):
+            for d in range(n_exp - 1, first - 1, -1):
                 body(d)
         else:
             lax.fori_loop(first, n_exp, lambda d, _: (body(d), 0)[1], 0)
@@ -224,7 +224,8 @@
             first, second = basis[t, 0, e], basis[t, 1, e]
             high = jnp.concatenate([w_high[first], w_high[second]], axis=0)
             low = jnp.concatenate([w_low[first], w_low[second]], axis=0)
-            got = dot(high, s_high) + dot(low, s_high) + dot(high, s_low)
+            both = dot(jnp.concatenate([high, low], axis=0), s_high)
+            got = both[:2 * TILE_ROWS] + both[2 * TILE_ROWS:] + dot(high, s_low)
             value = (1.0 - blend) * got[:TILE_ROWS] + blend * got[TILE_ROWS:]
             here = pl.ds(t * TILE_ROWS, TILE_ROWS)
             stage[e, here, :] = jnp.where(mask[e, here, :] == 1, value, SENTINEL)
@@ -248,7 +249,7 @@
             @pl.when(there(-a, -b))
             def _(c=c, at=at, a=a, b=b):
                 rim_copy(c, at, a, b).wait_recv()
-        lax.fori_loop(c * per, (c + 1) * per, warp, 0)
+        lax.fori_loop(c * per, (c + 1) * per, warp, 0, unroll=True)
         others(lambda who, c=c: stat_copy(c, who).start())
 
     def insert(state, value):
@@ -320,7 +321,7 @@
                     state = insert(state, recv[who, e])
             return state
 
-        state = lax.fori_loop(1, n_exp, take, state)
+        state = lax.fori_loop(1, n_exp, take, state, unroll=n_exp <= 8)
         total, number, l0, l1, l2, h0, h1, h2 = state
         value = (total - (l0 + l1 + l2) - (h0 + h1 + h2)) / (number - 6.0)
         own[...] = value
@@ -349,7 +350,9 @@
     low = w_low[...].reshape(n_bank * TILE_ROWS, wide)
     for t in range(tiles):
         s_high, s_low = pieces[t]
-        got = dot(high, s_high) + dot(low, s_high) + dot(high, s_low)
+        both = dot(jnp.concatenate([high, low], axis=0), s_high)
+        size = n_bank * TILE_ROWS
+        got = both[:size] + both[size:] + dot(high, s_low)
         conv[t * n_bank:(t + 1) * n_bank] = got.reshape(n_bank, TILE_ROWS, cols)
     coadd_out[...] = cpad[SUB:SUB + rows, LANES:LANES + cols]
 
@@ -365,7 +368,7 @@
             diff_out[e, here, :] = source - value
         return 0
 
-    lax.fori_loop(0, count, final, 0)
+    lax.fori_loop(0, count, final, 0, unroll=True)
 
     for c in range(chunks):
         for at, a, b in rims:

time: 24.7 us -> 23.6 us (0.955)
  Pallas kernels: 23.9 us -> 22.7 us
    pallas_call x1, Pallas kernels: 23.1 us -> 22 us  [on_device(): pl.pallas_call(functools.partial(kernel, n_exp, n_strip, n_band, chunks,...]
where the time goes in v3:
time: 23.6 us; the launch traced here: 23.4 us
  Pallas kernels  22.7 us (96%)
  between operations  0.64 us (3%)
    pallas_call x1, Pallas kernels, on_device(): pl.pallas_call(functools.partial(kernel, n_exp, n_strip, n_band, chunks,...  22 us
    pallas_call x1, Pallas kernels, on_device(): pl.pallas_call(functools.partial(deliver, count), out_shape=(jax.ShapeDty...  0.74 us

profile of v3, /device:TPU:0, one launch (start us, length us, event | category | flops | bytes accessed | tf_op | source)
XLA Modules:
  0.0 23.4 jit_solution(9680549060584952182)
XLA Ops:
  0.6 22.0 %shard_map.68 = (f32[32,256]{1,0:T(8,128)S(1)}, f32[8,32,256]{2,1,0:T(8,128)S(1)}) custom-call(f32[8,32,256]{2,1,0:T(8,128)} %images.1, s32[8,32,256]{2,1,0:T(8,128)} %mask_in.1, s32[2,2,8]{2,1,0:T(2,128)} %bitcast.2, s32[2,2,8]{2,1,0:T(2,128)} %bitcast.3, f32[16,81]{1,0:T(8,128)} %bank_in.1), custom_call_target="tpu_custom_call" | custom-call | tf_op jit(solution)/shard_map/pallas_call | solution.py:410
  22.6 0.7 %shard_map.69 = (f32[32,256]{1,0:T(8,128)}, f32[8,32,256]{2,1,0:T(8,128)}) custom-call(f32[32,256]{1,0:T(8,128)S(1)} %get-tuple-element.4.coadd, f32[8,32,256]{2,1,0:T(8,128)S(1)} %get-tuple-element.5.diff), custom_call_target="tpu_custom_call" | custom-call | tf_op jit(solution)/shard_map/pallas_call | solution.py:446
